TPU v7x, 32 devices: a whole 2x2x4 slice. The times are simulated.
32 devices in a mesh: groups: 2 (over y), dp: 4 (over z), fsdp: 4 (over x, core).
Axes of the slice: x: 2, y: 2, z: 4, core: 2. Of those that a mesh axis runs over, the one named last changes fastest.
Arguments:
- hidden: bfloat16 [4096, 5120], P(('groups', 'dp', 'fsdp')), parts along dimension 0, may hold values from -160 to 160
- queries: bfloat16 [4096, 2560], P(('groups', 'dp', 'fsdp')), parts along dimension 0, may hold values from -6 to 6
- source_table: bfloat16 [8, 5120], replicated, may hold values from -6 to 6
- norm_gain: float32 [5120], replicated, may hold values from 0.25 to 1.75
- key_value_weight: bfloat16 [5120, 1024], P(None, 'fsdp'), may hold values from -0.078125 to 0.078125
- value_projection_bias: float32 [512], replicated, may hold values from -3 to 3
- seq_lengths: int32 [8, 16], P(('groups', 'fsdp')), parts along dimension 0, may hold values from 1 to 32, as said below
- seq_sources: int32 [8, 16], P(('groups', 'fsdp')), parts along dimension 0, may hold values from 0 to 7
- dest_device: int32 [8, 16], P(('groups', 'fsdp')), parts along dimension 0, may hold values from 0 to 3, as said below
- dest_slot: int32 [8, 16], P(('groups', 'fsdp')), parts along dimension 0, may hold values from 0 to 96, as said below
- segment_ids: int32 [4096], P(('groups', 'dp', 'fsdp')), parts along dimension 0, may hold values from -1 to 127, as said below
Outputs:
- attention_out: bfloat16 [4096, 2560], P(('groups', 'dp', 'fsdp')), parts along dimension 0
There are 2 independent parts, one for each index of `groups`. A program takes and returns all parts, laid end to end along the dimension named above; an argument that names none is the same for every part. Nothing has to cross between parts.
Inputs may be any that keep to these rules, and one draw needn't show every extreme that they name: `seq_lengths`: the 4 slots of a block are packed from its first row in slot order; in every fsdp index there is one dp index all of whose received sequences have length 32. `dest_device`: each receiving block gets 4 sequences. `dest_slot`: the sequences sent to one block fill its first rows without gaps or intersections; in every fsdp index one receiving block is filled completely. `segment_ids`: -1 exactly on rows that receive nothing, which come last in a block; over a block's filled rows ids never fall, the last filled row has id 128 - 1, and a document lies within one sequence.
All inputs are finite; a program needn't handle non-finite values.
Results may differ from a plain program's by a relative error of at most 0.0056.
Values may be sent and summed in bfloat16 or wider, within the bound.
A program may use at most 64 MiB of HBM per device.

v0:
```python
import jax
import jax.numpy as jnp
from jax import lax
from jax.sharding import PartitionSpec as P

HEAD_SIZE = 128
QUERY_HEADS = 20
KEY_VALUE_HEADS = 4
SOURCES = 8
SEQS = 4


epsilon = 1e-06


def for_sending(shard):

    def short(part):
        return part.astype(jnp.bfloat16) if part.dtype == jnp.float32 else part

    return jax.tree.map(short, shard)


def source_rows(lengths, targets, offsets, input_rows):
    devices = lengths.shape[0] // SEQS
    grid = lengths.reshape(devices, SEQS)
    starts = (jnp.cumsum(grid, axis=1) - grid).reshape(-1)
    owners = jnp.arange(devices * SEQS) // SEQS
    src_base = owners * input_rows + starts
    dst_base = targets * input_rows + offsets
    places = jnp.arange(devices * input_rows)
    inside = (places[:, None] >= dst_base[None, :]) & (
        places[:, None] < (dst_base + lengths)[None, :]
    )
    shifts = jnp.sum(jnp.where(inside, (src_base - dst_base)[None, :], 0), axis=1)
    alive_mask = jnp.any(inside, axis=1)
    return (jnp.where(alive_mask, places + shifts, 0), alive_mask)


def normalize(hidden_rows, table, gain, lengths, tags):
    input_rows = hidden_rows.shape[0]
    starts = jnp.cumsum(lengths) - lengths
    places = jnp.arange(input_rows)
    inside = (places[:, None] >= starts[None, :]) & (places[:, None] < (starts + lengths)[None, :])
    kinds = jnp.arange(SOURCES)
    picks = jnp.any(inside[:, :, None] & (tags[None, :, None] == kinds[None, None, :]), axis=1)
    summed = hidden_rows.astype(jnp.float32) + jnp.dot(
        picks.astype(table.dtype), table, preferred_element_type=jnp.float32
    )
    scale = lax.rsqrt(jnp.mean(summed * summed, axis=1, keepdims=True) + epsilon)
    return (summed * scale * gain).astype(jnp.bfloat16)


def attend(query_matrix, key_value_rows, segments, alive_mask):
    input_rows = query_matrix.shape[0]
    query_groups = QUERY_HEADS // KEY_VALUE_HEADS
    quadruples = query_matrix.reshape(input_rows, KEY_VALUE_HEADS, query_groups, HEAD_SIZE)
    key_rows = key_value_rows[:, : KEY_VALUE_HEADS * HEAD_SIZE].reshape(
        input_rows, KEY_VALUE_HEADS, HEAD_SIZE
    )
    value_rows = key_value_rows[:, KEY_VALUE_HEADS * HEAD_SIZE :].reshape(
        input_rows, KEY_VALUE_HEADS, HEAD_SIZE
    )
    scores = jnp.einsum(
        "tkgd,skd->kgts", quadruples, key_rows, preferred_element_type=jnp.float32
    ) * HEAD_SIZE ** (-0.5)
    places = jnp.arange(input_rows)
    allowed = (segments[:, None] == segments[None, :]) & (places[None, :] <= places[:, None])
    weights = jnp.where(allowed[None, None], jnp.exp(scores), 0.0)
    totals = jnp.sum(weights, axis=3)
    mixed = jnp.einsum(
        "kgts,skd->tkgd",
        weights.astype(jnp.bfloat16),
        value_rows,
        preferred_element_type=jnp.float32,
    )
    mixed = mixed / jnp.transpose(totals, (2, 0, 1))[..., None]
    return jnp.where(
        alive_mask[:, None], mixed.reshape(input_rows, QUERY_HEADS * HEAD_SIZE), 0.0
    ).astype(jnp.bfloat16)


def relocate(blocks, src_index, alive_mask):
    spread = (
        lax.all_to_all(blocks[0], "dp", split_axis=1, concat_axis=0, tiled=True),
        lax.all_to_all(blocks[1], "dp", split_axis=1, concat_axis=0, tiled=True),
    )
    picked = tuple(
        (
            jnp.where(
                alive_mask[:, None], jnp.take(block, src_index, axis=0), jnp.zeros((), block.dtype)
            )
            for block in spread
        )
    )
    return jax.tree.map(
        lambda part, own: part.astype(own.dtype),
        lax.all_to_all(for_sending(picked), "dp", split_axis=0, concat_axis=1, tiled=True),
        picked,
    )


def project(token_block, key_value_weight, complete_bias):
    product = jnp.dot(
        token_block,
        lax.all_gather(key_value_weight, "fsdp", axis=1, tiled=True),
        preferred_element_type=jnp.float32,
    )
    total = product + complete_bias[None, :]
    return total.astype(jnp.bfloat16)


def body(
    hidden,
    queries,
    source_table,
    norm_gain,
    key_value_weight,
    value_projection_bias,
    seq_lengths,
    seq_sources,
    dest_device,
    dest_slot,
    segment_ids,
):
    input_rows = hidden.shape[0]
    lengths = seq_lengths[0]
    tags = seq_sources[0]
    targets = dest_device[0]
    offsets = dest_slot[0]
    position = lax.axis_index("dp")
    own_lengths = lax.dynamic_slice_in_dim(lengths, position * SEQS, SEQS)
    own_tags = lax.dynamic_slice_in_dim(tags, position * SEQS, SEQS)
    normed = normalize(hidden, source_table, norm_gain, own_lengths, own_tags)
    src_index, alive_mask = source_rows(lengths, targets, offsets, input_rows)
    own_living = lax.dynamic_slice_in_dim(alive_mask, position * input_rows, input_rows)
    complete_bias = jnp.concatenate(
        [jnp.zeros((KEY_VALUE_HEADS * HEAD_SIZE,), jnp.float32), value_projection_bias]
    )
    moved, relocated_queries = relocate((normed, queries), src_index, alive_mask)
    key_value_rows = project(moved, key_value_weight, complete_bias)
    return attend(relocated_queries, key_value_rows, segment_ids, own_living)


def solution(mesh):
    placed = (
        P(("groups", "dp", "fsdp"), None),
        P(("groups", "dp", "fsdp"), None),
        P(),
        P(),
        P(None, "fsdp"),
        P(),
        P(("groups", "fsdp"), None),
        P(("groups", "fsdp"), None),
        P(("groups", "fsdp"), None),
        P(("groups", "fsdp"), None),
        P(("groups", "dp", "fsdp")),
    )
    return jax.shard_map(
        body,
        mesh=mesh,
        in_specs=placed,
        out_specs=P(("groups", "dp", "fsdp"), None),
        check_vma=False,
    )
```

profile of v0, /device:TPU:0, one launch (start us, length us, event | category | flops | bytes accessed | tf_op | source)
XLA Modules:
  0.0 131.7 jit_solution(17548493394455407540)
XLA Ops:
  6.5 0.0 copy-start
  6.5 0.0 copy-start.6
  6.5 0.0 copy-start.9
  6.5 0.0 copy-start.1
  6.5 0.0 all-gather.2.cloned.1.call-start
  6.6 0.7 all-gather.2.cloned.1.call-update
  7.3 0.0 copy-done.6
  7.3 0.1 fusion.17
  7.4 0.2 reduce-window.4
  7.5 0.0 copy-done.9
  7.5 0.1 fusion.15
  7.6 0.1 iota_compare_fusion.3
  7.7 0.1 fusion.11
  7.8 0.1 and_reduce_fusion
  7.9 0.0 copy-done
  7.9 0.1 copy-done.1
  7.9 0.0 copy-start.3
  7.9 0.6 multiply_reduce_fusion
  8.6 0.1 copy-done.3
  8.7 0.3 multiply_convert_fusion
  9.0 1.2 copy.60
  10.2 0.0 copy-start.2
  10.2 6.4 %all-to-all-start = ((bf16[128,4,1280]{2,0,1:T(8,128)(2,1)}), bf16[128,4,1280]{2,0,1:T(8,128)(2,1)S(1)}, u32[]{:S(2)}, u32[]{:S(2)}) async-start(bf16[128,4,1280]{2,0,1:T(8,128)(2,1)} %bitcast.72), calls=%async_computation | async-start | bytes 2621440 | tf_op jit(solution)/shard_map/all_to_all | solution.py:85
  16.6 0.0 copy-start.7
  16.6 0.0 copy-start.8
  16.6 0.5 broadcast.207
  17.1 0.7 reduce.3
  17.8 0.1 reshape_squeeze.3
  17.9 0.2 reduce_window_sum.20
  18.1 0.1 reduce_window_sum.21
  18.1 0.0 copy-done.2
  18.1 0.9 copy.61
  19.0 0.0 copy-done.7
  19.0 0.0 copy-done.8
  19.1 0.1 fusion.9
  19.2 0.1 select_reduce_fusion
  19.2 28.7 %all-to-all-done = bf16[128,4,1280]{2,0,1:T(8,128)(2,1)S(1)} async-done(((bf16[128,4,1280]{2,0,1:T(8,128)(2,1)}), bf16[128,4,1280]{2,0,1:T(8,128)(2,1)S(1)}, u32[]{:S(2)}, u32[]{:S(2)}) %all-to-all-start) | async-done | bytes 1310752 | tf_op jit(solution)/shard_map/all_to_all | solution.py:85
  47.9 3.5 %all-to-all-start.2 = ((bf16[128,4,640]{2,0,1:T(8,128)(2,1)}), bf16[128,4,640]{2,0,1:T(8,128)(2,1)S(1)}, u32[]{:S(2)}, u32[]{:S(2)}) async-start(bf16[128,4,640]{2,0,1:T(8,128)(2,1)} %bitcast.73), calls=%async_computation.2 | async-start | bytes 1310720 | tf_op jit(solution)/shard_map/all_to_all | solution.py:86
  51.5 2.1 %gather_fusion = bf16[512,1280]{1,0:T(8,128)(2,1)S(1)} fusion(bf16[512,1280]{1,0:T(8,128)(2,1)S(1)} %bitcast.74, s32[1024]{0:T(1024)S(1)} %pad_clamp_fusion), kind=kCustom, calls=%fused_computation | custom fusion | bytes 2623488 | tf_op jit(solution)/shard_map/jit(_take)/gather | solution.py:91
  53.6 0.8 copy.37
  54.4 1.2 select_select_fusion
  55.6 12.6 %all-to-all-done.2 = bf16[128,4,640]{2,0,1:T(8,128)(2,1)S(1)} async-done(((bf16[128,4,640]{2,0,1:T(8,128)(2,1)}), bf16[128,4,640]{2,0,1:T(8,128)(2,1)S(1)}, u32[]{:S(2)}, u32[]{:S(2)}) %all-to-all-start.2) | async-done | bytes 655392 | tf_op jit(solution)/shard_map/all_to_all | solution.py:86
  68.2 3.5 %all-to-all-start.1 = ((bf16[4,128,1280]{1,2,0:T(8,128)(2,1)}), bf16[4,128,1280]{1,2,0:T(8,128)(2,1)S(1)}, u32[]{:S(2)}, u32[]{:S(2)}) async-start(bf16[4,128,1280]{1,2,0:T(8,128)(2,1)} %select_select_fusion), calls=%async_computation.1 | async-start | bytes 2621440 | tf_op jit(solution)/shard_map/all_to_all | solution.py:98
  71.8 2.0 %gather_fusion.1 = bf16[512,640]{1,0:T(8,128)(2,1)S(1)} fusion(bf16[512,640]{1,0:T(8,128)(2,1)S(1)} %bitcast.75, s32[1024]{0:T(1024)S(1)} %pad_clamp_fusion), kind=kCustom, calls=%fused_computation.1 | custom fusion | bytes 1312768 | tf_op jit(solution)/shard_map/jit(_take)/gather | solution.py:91
  73.8 0.3 copy.39
  74.1 0.0 copy-start.4
  74.1 0.0 copy-start.5
  74.1 0.9 select_select_fusion.1
  75.1 27.5 %all-to-all-done.1 = bf16[4,128,1280]{1,2,0:T(8,128)(2,1)S(1)} async-done(((bf16[4,128,1280]{1,2,0:T(8,128)(2,1)}), bf16[4,128,1280]{1,2,0:T(8,128)(2,1)S(1)}, u32[]{:S(2)}, u32[]{:S(2)}) %all-to-all-start.1) | async-done | bytes 1310752 | tf_op jit(solution)/shard_map/all_to_all | solution.py:98
  102.6 3.5 %all-to-all-start.3 = ((bf16[4,128,640]{1,2,0:T(8,128)(2,1)}), bf16[4,128,640]{1,2,0:T(8,128)(2,1)S(1)}, u32[]{:S(2)}, u32[]{:S(2)}) async-start(bf16[4,128,640]{1,2,0:T(8,128)(2,1)} %select_select_fusion.1), calls=%async_computation.3 | async-start | bytes 1310720 | tf_op jit(solution)/shard_map/all_to_all | solution.py:98
  106.0 0.0 copy-done.4
  106.1 0.1 fusion.7
  106.2 0.1 dynamic_slice.9
  106.2 0.0 copy-done.5
  106.2 0.0 all-gather.2.cloned.1.call-done
  106.3 5.5 %fusion.4 = bf16[128,1024]{1,0:T(8,128)(2,1)S(1)} fusion(bf16[128,5120]{0,1:T(8,128)(2,1)S(1)} %bitcast.76, bf16[5120,1024]{1,0:T(8,128)(2,1)} %all-gather.2.cloned.1.call-done, f32[1024]{0:T(1024)S(1)} %concatenate.3), kind=kOutput, calls=%fused_computation.15 | convolution fusion | flops 1342439424 | bytes 12062720 | tf_op jit(solution)/shard_map/dot_general | solution.py:104
  111.9 0.1 copy.49
  112.0 10.8 %all-to-all-done.3 = bf16[4,128,640]{1,2,0:T(8,128)(2,1)S(1)} async-done(((bf16[4,128,640]{1,2,0:T(8,128)(2,1)}), bf16[4,128,640]{1,2,0:T(8,128)(2,1)S(1)}, u32[]{:S(2)}, u32[]{:S(2)}) %all-to-all-start.3) | async-done | bytes 655392 | tf_op jit(solution)/shard_map/all_to_all | solution.py:98
  122.8 0.5 fusion.20
  123.3 0.3 fusion.3
  123.6 0.2 copy.44
  123.9 1.0 select_convert_fusion
  (8 shorter events, 0.1 us)
Async XLA Ops:
  6.5 1.3 %copy-start = (bf16[8,5120]{1,0:T(8,128)(2,1)S(1)}, bf16[8,5120]{1,0:T(8,128)(2,1)}, u32[]{:S(2)}) copy-start(bf16[8,5120]{1,0:T(8,128)(2,1)} %param.13) | copy-start | bytes 245764
  6.5 0.7 copy-start.6
  6.5 1.0 copy-start.9
  6.5 1.4 %copy-start.1 = (bf16[128,5120]{1,0:T(8,128)(2,1)S(1)}, bf16[128,5120]{1,0:T(8,128)(2,1)}, u32[]{:S(2)}) copy-start(bf16[128,5120]{1,0:T(8,128)(2,1)} %param.11) | copy-start | bytes 3932164
  6.5 99.7 %all-gather.2.cloned.1.call-start = ((), (), s32[]{:S(2)}) async-start(), calls=%async_computation.4 | async-start | bytes 13107200 | tf_op jit(solution)/shard_map/all_gather | solution.py:106
  7.9 0.7 copy-start.3
  10.2 8.0 %copy-start.2 = (bf16[128,2560]{1,0:T(8,128)(2,1)S(1)}, bf16[128,2560]{1,0:T(8,128)(2,1)}, u32[]{:S(2)}) copy-start(bf16[128,2560]{1,0:T(8,128)(2,1)} %param.12) | copy-start | bytes 1966084
  10.2 37.8 %all-to-all-start = ((bf16[128,4,1280]{2,0,1:T(8,128)(2,1)}), bf16[128,4,1280]{2,0,1:T(8,128)(2,1)S(1)}, u32[]{:S(2)}, u32[]{:S(2)}) async-start(bf16[128,4,1280]{2,0,1:T(8,128)(2,1)} %bitcast.72), calls=%async_computation | async-start | bytes 2621440 | tf_op jit(solution)/shard_map/all_to_all | solution.py:85
  16.6 2.4 %copy-start.7 = (s32[1,16]{1,0:T(1,128)S(1)}, s32[1,16]{1,0:T(1,128)}, u32[]{:S(2)}) copy-start(s32[1,16]{1,0:T(1,128)} %param.20) | copy-start | bytes 196
  16.6 2.4 %copy-start.8 = (s32[1,16]{1,0:T(1,128)S(1)}, s32[1,16]{1,0:T(1,128)}, u32[]{:S(2)}) copy-start(s32[1,16]{1,0:T(1,128)} %param.19) | copy-start | bytes 196
  47.9 20.3 %all-to-all-start.2 = ((bf16[128,4,640]{2,0,1:T(8,128)(2,1)}), bf16[128,4,640]{2,0,1:T(8,128)(2,1)S(1)}, u32[]{:S(2)}, u32[]{:S(2)}) async-start(bf16[128,4,640]{2,0,1:T(8,128)(2,1)} %bitcast.73), calls=%async_computation.2 | async-start | bytes 1310720 | tf_op jit(solution)/shard_map/all_to_all | solution.py:86
  68.2 34.3 %all-to-all-start.1 = ((bf16[4,128,1280]{1,2,0:T(8,128)(2,1)}), bf16[4,128,1280]{1,2,0:T(8,128)(2,1)S(1)}, u32[]{:S(2)}, u32[]{:S(2)}) async-start(bf16[4,128,1280]{1,2,0:T(8,128)(2,1)} %select_select_fusion), calls=%async_computation.1 | async-start | bytes 2621440 | tf_op jit(solution)/shard_map/all_to_all | solution.py:98
  74.1 31.9 %copy-start.4 = (s32[128]{0:T(128)S(1)}, s32[128]{0:T(128)}, u32[]{:S(2)}) copy-start(s32[128]{0:T(128)} %param.21) | copy-start | bytes 1540
  74.1 32.1 %copy-start.5 = (f32[512]{0:T(512)S(1)}, f32[512]{0:T(512)}, u32[]{:S(2)}) copy-start(f32[512]{0:T(512)} %param.16) | copy-start | bytes 6148
  102.6 20.2 %all-to-all-start.3 = ((bf16[4,128,640]{1,2,0:T(8,128)(2,1)}), bf16[4,128,640]{1,2,0:T(8,128)(2,1)S(1)}, u32[]{:S(2)}, u32[]{:S(2)}) async-start(bf16[4,128,640]{1,2,0:T(8,128)(2,1)} %select_select_fusion.1), calls=%async_computation.3 | async-start | bytes 1310720 | tf_op jit(solution)/shard_map/all_to_all | solution.py:98
Sparse Core Ops, SparseCore 0:
  8.9 74.2 all-gather.1
where the time goes:
time: 132 us
  waiting for transfers between devices  80.3 us (61%)
  starting transfers between devices  17 us (13%)
  between operations  13.6 us (10%)
  local copies, waits for them, and re-layouts  8.78 us (7%)
  matrix products  6.95 us (5%)
  other arithmetic  5.13 us (4%)
    all_to_all x2, waiting for transfers between devices, relocate(): lax.all_to_all(for_sending(picked), 'dp', split_axis=0, concat_axis=1, ti...  38.3 us
    all_to_all x1, waiting for transfers between devices, relocate(): lax.all_to_all(blocks[0], 'dp', split_axis=1, concat_axis=0, tiled=True)  28.7 us
    all_to_all x1, waiting for transfers between devices, relocate(): lax.all_to_all(blocks[1], 'dp', split_axis=1, concat_axis=0, tiled=True)  12.6 us
    all_to_all x2, starting transfers between devices, relocate(): lax.all_to_all(for_sending(picked), 'dp', split_axis=0, concat_axis=1, ti...  7.02 us
    all_to_all x1, starting transfers between devices, relocate(): lax.all_to_all(blocks[0], 'dp', split_axis=1, concat_axis=0, tiled=True)  6.45 us
    dot_general x1, matrix products, project(): jnp.dot(token_block, lax.all_gather(key_value_weight, 'fsdp', axis=1, til...  5.53 us
    gather x4, local copies, waits for them, and re-layouts, relocate(): jnp.take(block, src_index, axis=0)  5.26 us
    all_to_all x1, starting transfers between devices, relocate(): lax.all_to_all(blocks[1], 'dp', split_axis=1, concat_axis=0, tiled=True)  3.48 us
  transfers between devices with their start and end apart: 5, of which 4 were waited for; matrix products, arithmetic and copies ran while one was open for 14% of the time, Pallas kernels for 0%

commit v1 on v0

--- a/solution.py
+++ b/solution.py
@@ -1,6 +1,10 @@
+import functools
+
 import jax
 import jax.numpy as jnp
 from jax import lax
+from jax.experimental import pallas as pl
+from jax.experimental.pallas import tpu as pltpu
 from jax.sharding import PartitionSpec as P
 
 HEAD_SIZE = 128
@@ -142,6 +146,403 @@
     return attend(relocated_queries, key_value_rows, segment_ids, own_living)
 
 
+MESH_ID = pl.DeviceIdType.MESH
+CHUNKS = 4
+
+
+def fused_kernel(
+    n_dp,
+    lengths_ref,
+    tags_ref,
+    targets_ref,
+    offsets_ref,
+    hidden_ref,
+    queries_ref,
+    table_ref,
+    gain_ref,
+    weight_ref,
+    bias_ref,
+    seg_row_ref,
+    seg_col_ref,
+    out_ref,
+    weight,
+    rows_held,
+    kv_own,
+    kv_first,
+    q_first,
+    q_perm,
+    kv_perm,
+    q_last,
+    kv_last,
+    weight_sem,
+    x_send,
+    x_recv,
+    c_send,
+    c_recv,
+    f_send,
+    f_recv,
+    q1_send,
+    q1_recv,
+    kv1_send,
+    kv1_recv,
+    q2_send,
+    q2_recv,
+    kv2_send,
+    kv2_recv,
+):
+    rows = hidden_ref.shape[0]
+    part = rows // CHUNKS
+    every = n_dp * rows
+    q_width = queries_ref.shape[1] // n_dp
+    i = lax.axis_index("dp")
+    f = lax.axis_index("fsdp")
+    core_mate = f + 1 - 2 * lax.rem(f, 2)
+    x_mate = lax.rem(f + 2, 4)
+    diagonal = lax.rem(core_mate + 2, 4)
+    holders = (f, core_mate, x_mate, diagonal)
+
+    def remote(src, dst, send, recv, dp, fsdp):
+        return pltpu.make_async_remote_copy(
+            src_ref=src,
+            dst_ref=dst,
+            send_sem=send,
+            recv_sem=recv,
+            device_id={"dp": dp, "fsdp": fsdp},
+            device_id_type=MESH_ID,
+        )
+
+    load_weight = pltpu.make_async_copy(weight_ref, weight, weight_sem)
+    load_weight.start()
+    barrier = pltpu.get_barrier_semaphore()
+    for a in range(n_dp):
+        for b in range(4):
+            if a or b:
+                pl.semaphore_signal(
+                    barrier,
+                    inc=1,
+                    device_id={"dp": lax.rem(i + a, n_dp), "fsdp": lax.rem(f + b, 4)},
+                    device_id_type=MESH_ID,
+                )
+
+    lengths = [lengths_ref[0, s] for s in range(n_dp * SEQS)]
+
+    def norm_part(c):
+        place = lax.broadcasted_iota(jnp.int32, (part, 1), 0) + c * part
+        kind = jnp.full((part, 1), -1, jnp.int32)
+        start = 0
+        for s in range(SEQS):
+            own_length = lengths_ref[0, i * SEQS + s]
+            inside = (place >= start) & (place < start + own_length)
+            kind = jnp.where(inside, tags_ref[0, i * SEQS + s], kind)
+            start = start + own_length
+        kinds = lax.broadcasted_iota(jnp.int32, (part, SOURCES), 1)
+        picks = jnp.where(kinds == kind, 1.0, 0.0).astype(jnp.bfloat16)
+        own = pl.ds(c * part, part)
+        summed = hidden_ref[own, :].astype(jnp.float32) + jnp.dot(
+            picks, table_ref[...], preferred_element_type=jnp.float32
+        )
+        scale = lax.rsqrt(jnp.mean(summed * summed, axis=1, keepdims=True) + epsilon)
+        rows_held[0, own, :] = (summed * scale * gain_ref[...]).astype(jnp.bfloat16)
+
+    def x_copy(c):
+        own = pl.ds(c * part, part)
+        return remote(
+            rows_held.at[0, own], rows_held.at[2, own], x_send.at[c], x_recv.at[c], i, x_mate
+        )
+
+    def c_copy(c):
+        own = pl.ds(c * part, part)
+        return remote(
+            rows_held.at[0, own], rows_held.at[1, own], c_send.at[c], c_recv.at[c], i, core_mate
+        )
+
+    def f_copy(c):
+        own = pl.ds(c * part, part)
+        return remote(
+            rows_held.at[2, own], rows_held.at[3, own], f_send.at[c], f_recv.at[c], i, core_mate
+        )
+
+    def q1_copy(o):
+        head = lax.rem(i + o, n_dp)
+        cols = pl.ds(pl.multiple_of(head * q_width, 128), q_width)
+        return remote(
+            queries_ref.at[:, cols], q_first.at[i], q1_send.at[o], q1_recv.at[o], head, f
+        )
+
+    norm_part(0)
+    pl.semaphore_wait(barrier, n_dp * 4 - 1)
+    x_copy(0).start()
+    c_copy(0).start()
+    q1_own = pltpu.make_async_copy(
+        queries_ref.at[:, pl.ds(pl.multiple_of(i * q_width, 128), q_width)],
+        q_first.at[i],
+        q1_recv.at[0],
+    )
+    q1_own.start()
+    for o in range(1, n_dp):
+        q1_copy(o).start()
+    for c in range(1, CHUNKS):
+        norm_part(c)
+        x_copy(c).start()
+        c_copy(c).start()
+
+    kind_of_half = f // 2
+    value_at = pl.multiple_of(lax.rem(f, 2) * 256, 256)
+    bias = bias_ref[:, pl.ds(value_at, 256)] * kind_of_half.astype(jnp.float32)
+
+    def project_part(slot, first, count):
+        own = pl.ds(first, count)
+        product = jnp.dot(
+            rows_held[slot, own, :], weight[...], preferred_element_type=jnp.float32
+        )
+        kv = (product + bias).astype(jnp.bfloat16)
+        for half in range(2):
+            kv_own[slot, half, own, :] = kv[:, half * HEAD_SIZE : (half + 1) * HEAD_SIZE]
+
+    def kv1_copy(slot, half, first, count):
+        head = 2 * lax.rem(f, 2) + half
+        landing = pl.ds(pl.multiple_of(i * rows + first, count), count)
+        return remote(
+            kv_own.at[slot, half, pl.ds(first, count)],
+            kv_first.at[kind_of_half, landing],
+            kv1_send.at[slot, half],
+            kv1_recv.at[i, kind_of_half],
+            head,
+            holders[slot],
+        )
+
+    def send_kv(slot, first, count):
+        for half in range(2):
+            if slot == 0:
+                head = 2 * lax.rem(f, 2) + half
+
+                @pl.when(head != i)
+                def _():
+                    kv1_copy(slot, half, first, count).start()
+
+                @pl.when(head == i)
+                def _():
+                    pltpu.make_async_copy(
+                        kv_own.at[slot, half, pl.ds(first, count)],
+                        kv_first.at[kind_of_half, pl.ds(pl.multiple_of(i * rows, rows), rows)],
+                        kv1_recv.at[i, kind_of_half],
+                    ).start()
+
+            else:
+                kv1_copy(slot, half, first, count).start()
+
+    load_weight.wait()
+    project_part(0, 0, rows)
+    send_kv(0, 0, rows)
+
+    lane = lax.broadcasted_iota(jnp.int32, (1, every), 1)
+    target = jnp.full((1, every), -1, jnp.int32)
+    for a in range(n_dp):
+        start = a * rows
+        for s in range(a * SEQS, (a + 1) * SEQS):
+            inside = (lane >= start) & (lane < start + lengths[s])
+            base = targets_ref[0, s] * rows + offsets_ref[0, s] - start
+            target = jnp.where(inside, lane + base, target)
+            start = start + lengths[s]
+
+    def chosen(block):
+        place = lax.broadcasted_iota(jnp.int32, (rows, every), 0) + block * rows
+        return jnp.where(place == target, 1.0, 0.0).astype(jnp.bfloat16)
+
+    def q2_copy(o):
+        d = lax.rem(i + o, n_dp)
+        return remote(
+            q_perm.at[o], q_last.at[i], q2_send.at[o], q2_recv.at[o], d, f
+        )
+
+    def kv2_copy(o):
+        d = lax.rem(i + o, n_dp)
+        return remote(
+            kv_perm.at[o], kv_last.at[i], kv2_send.at[o], kv2_recv.at[o], d, f
+        )
+
+    def move_queries():
+        q1_own.wait()
+        for o in range(1, n_dp):
+            q1_copy(o).wait_recv()
+        full = q_first[...].reshape(every, q_width)
+        for o in (2, 3, 1, 0):
+            moved = jnp.dot(
+                chosen(lax.rem(i + o, n_dp)), full, preferred_element_type=jnp.float32
+            ).astype(jnp.bfloat16)
+            if o:
+                q_perm[o] = moved
+                q2_copy(o).start()
+            else:
+                q_last[i] = moved
+
+    for c in range(CHUNKS):
+        c_copy(c).wait_recv()
+    project_part(1, 0, rows)
+    send_kv(1, 0, rows)
+
+    for c in range(CHUNKS):
+        x_copy(c).wait_recv()
+        f_copy(c).start()
+        if c == CHUNKS // 2:
+            move_queries()
+        project_part(2, c * part, part)
+        send_kv(2, c * part, part)
+        f_copy(c).wait_recv()
+        project_part(3, c * part, part)
+        send_kv(3, c * part, part)
+
+    for a in range(n_dp):
+        for t in range(2):
+            landing = kv_first.at[t, pl.ds(a * rows, rows)]
+            remote(
+                landing, landing, kv1_send.at[0, 0], kv1_recv.at[a, t], i, x_mate
+            ).wait_recv()
+    for o in (2, 3, 1, 0):
+        pick = chosen(lax.rem(i + o, n_dp))
+        for t in range(2):
+            moved = jnp.dot(pick, kv_first[t], preferred_element_type=jnp.float32).astype(
+                jnp.bfloat16
+            )
+            if o:
+                kv_perm[o, t] = moved
+            else:
+                kv_last[i, t] = moved
+        if o:
+            kv2_copy(o).start()
+
+    seg_col = seg_col_ref[...]
+    row_at = lax.broadcasted_iota(jnp.int32, (rows, rows), 0)
+    col_at = lax.broadcasted_iota(jnp.int32, (rows, rows), 1)
+    allowed = (seg_col == seg_row_ref[...]) & (col_at <= row_at)
+    alive = seg_col >= 0
+    heads = QUERY_HEADS // KEY_VALUE_HEADS
+
+    def attend_head(k):
+        block = q_last[k]
+        stacked = jnp.concatenate(
+            [block[:, h * HEAD_SIZE : (h + 1) * HEAD_SIZE] for h in range(heads)], axis=0
+        )
+        scores = lax.dot_general(
+            stacked,
+            kv_last[k, 0],
+            (((1,), (1,)), ((), ())),
+            preferred_element_type=jnp.float32,
+        ) * HEAD_SIZE ** (-0.5)
+        scores = scores.reshape(heads, rows, rows)
+        weights = jnp.where(allowed[None], jnp.exp(scores), 0.0)
+        totals = jnp.sum(weights, axis=2, keepdims=True)
+        mixed = jnp.dot(
+            weights.astype(jnp.bfloat16).reshape(heads * rows, rows),
+            kv_last[k, 1],
+            preferred_element_type=jnp.float32,
+        ).reshape(heads, rows, HEAD_SIZE)
+        mixed = jnp.where(alive[None], mixed / totals, 0.0).astype(jnp.bfloat16)
+        for h in range(heads):
+            at = pl.multiple_of((k * heads + h) * HEAD_SIZE, HEAD_SIZE)
+            out_ref[:, pl.ds(at, HEAD_SIZE)] = mixed[h]
+
+    attend_head(i)
+    for o in (1, 3, 2):
+        q2_copy(o).wait_recv()
+        kv2_copy(o).wait_recv()
+        attend_head(lax.rem(i + n_dp - o, n_dp))
+
+    for c in range(CHUNKS):
+        x_copy(c).wait_send()
+        c_copy(c).wait_send()
+        f_copy(c).wait_send()
+    for o in range(1, n_dp):
+        q1_copy(o).wait_send()
+        q2_copy(o).wait_send()
+        kv2_copy(o).wait_send()
+    for half in range(2):
+        for slot in range(1, 4):
+            kv1_copy(slot, half, 0, rows).wait_send()
+
+        @pl.when(2 * lax.rem(f, 2) + half != i)
+        def _():
+            kv1_copy(0, half, 0, rows).wait_send()
+
+
+def fused_body(
+    n_dp,
+    hidden,
+    queries,
+    source_table,
+    norm_gain,
+    key_value_weight,
+    value_projection_bias,
+    seq_lengths,
+    seq_sources,
+    dest_device,
+    dest_slot,
+    segment_ids,
+):
+    rows, model = hidden.shape
+    q_width = queries.shape[1] // n_dp
+    columns = key_value_weight.shape[1]
+    every = n_dp * rows
+    vmem = pl.BlockSpec(memory_space=pltpu.VMEM)
+    smem = pl.BlockSpec(memory_space=pltpu.SMEM)
+    anywhere = pl.BlockSpec(memory_space=pl.ANY)
+    bf16 = jnp.bfloat16
+    dma = pltpu.SemaphoreType.DMA
+    return pl.pallas_call(
+        functools.partial(fused_kernel, n_dp),
+        out_shape=jax.ShapeDtypeStruct(queries.shape, bf16),
+        in_specs=[smem] * 4 + [vmem, anywhere, vmem, vmem, anywhere, vmem, vmem, vmem],
+        out_specs=vmem,
+        scratch_shapes=[
+            pltpu.VMEM((model, columns), bf16),
+            pltpu.VMEM((4, rows, model), bf16),
+            pltpu.VMEM((4, 2, rows, HEAD_SIZE), bf16),
+            pltpu.VMEM((2, every, HEAD_SIZE), bf16),
+            pltpu.VMEM((n_dp, rows, q_width), bf16),
+            pltpu.VMEM((n_dp, rows, q_width), bf16),
+            pltpu.VMEM((n_dp, 2, rows, HEAD_SIZE), bf16),
+            pltpu.VMEM((n_dp, rows, q_width), bf16),
+            pltpu.VMEM((n_dp, 2, rows, HEAD_SIZE), bf16),
+            dma,
+            dma((CHUNKS,)),
+            dma((CHUNKS,)),
+            dma((CHUNKS,)),
+            dma((CHUNKS,)),
+            dma((CHUNKS,)),
+            dma((CHUNKS,)),
+            dma((n_dp,)),
+            dma((n_dp,)),
+            dma((4, 2)),
+            dma((n_dp, 2)),
+            dma((n_dp,)),
+            dma((n_dp,)),
+            dma((n_dp,)),
+            dma((n_dp,)),
+        ],
+        compiler_params=pltpu.CompilerParams(
+            collective_id=0, has_side_effects=True, vmem_limit_bytes=40 * 2**20
+        ),
+        cost_estimate=pl.CostEstimate(
+            flops=2 * 4 * rows * model * columns,
+            bytes_accessed=8 * 2**20,
+            transcendentals=QUERY_HEADS * rows * rows,
+        ),
+    )(
+        seq_lengths,
+        seq_sources,
+        dest_device,
+        dest_slot,
+        hidden,
+        queries,
+        source_table,
+        norm_gain[None, :],
+        key_value_weight,
+        value_projection_bias[None, :],
+        segment_ids[None, :],
+        segment_ids[:, None],
+    )
+
+
 def solution(mesh):
     placed = (
         P(("groups", "dp", "fsdp"), None),
@@ -156,8 +557,10 @@
         P(("groups", "fsdp"), None),
         P(("groups", "dp", "fsdp")),
     )
+    n_dp = mesh.shape["dp"]
+    heads_fit = n_dp == KEY_VALUE_HEADS and mesh.shape["fsdp"] == 4
     return jax.shard_map(
-        body,
+        functools.partial(fused_body, n_dp) if heads_fit else body,
         mesh=mesh,
         in_specs=placed,
         out_specs=P(("groups", "dp", "fsdp"), None),

time: 132 us -> 68.6 us (0.52)
  waiting for transfers between devices: 80.3 us -> 0 us
  Pallas kernels: 0 us -> 56.8 us
  starting transfers between devices: 17 us -> 0 us
  between operations: 13.6 us -> 0.03 us
  matrix products: 6.95 us -> 0 us
  other arithmetic: 5.13 us -> 0 us
  local copies, waits for them, and re-layouts: 8.78 us -> 11.3 us
    all_to_all x4 -> x0, waiting for transfers between devices: 79.6 us -> none  [the longest x2 38.3 us: relocate(): lax.all_to_all(for_sending(picked), 'dp', split_axis=0, concat_axis=1, ti...]
    pallas_call x0 -> x1, Pallas kernels: none -> 56.8 us  [fused_body(): pl.pallas_call(functools.partial(fused_kernel, n_dp), out_shape=jax.Shape...]
    all_to_all x4 -> x0, starting transfers between devices: 17 us -> none  [the longest x2 7.02 us: relocate(): lax.all_to_all(for_sending(picked), 'dp', split_axis=0, concat_axis=1, ti...]
    unnamed x21 -> x23, local copies, waits for them, and re-layouts: 0.7 us -> 10.5 us
    dot_general x4 -> x0, matrix products: 6.95 us -> none  [the longest x1 5.53 us: project(): jnp.dot(token_block, lax.all_gather(key_value_weight, 'fsdp', axis=1, til...]
    gather x4 -> x0, local copies, waits for them, and re-layouts: 5.26 us -> none  [relocate(): jnp.take(block, src_index, axis=0)]
    select_n x3 -> x0, other arithmetic: 2.16 us -> none  [the longest x2 2.15 us: relocate(): jnp.where(alive_mask[:, None], jnp.take(block, src_index, axis=0), jnp.ze...]
    all_to_all x2 -> x0, local copies, waits for them, and re-layouts: 2.06 us -> none  [the longest x1 1.16 us: relocate(): lax.all_to_all(blocks[0], 'dp', split_axis=1, concat_axis=0, tiled=True)]
  transfers between devices with their start and end apart: 5 -> 0, of which waited for: 4 -> 0; matrix products, arithmetic and copies ran while one was open for 14% -> 0% of each run, Pallas kernels for 0% -> 0%
where the time goes in v1:
time: 68.6 us; the launch traced here: 68.2 us
  Pallas kernels  56.8 us (83%)
  local copies, waits for them, and re-layouts  11.3 us (16%)
    pallas_call x1, Pallas kernels, fused_body(): pl.pallas_call(functools.partial(fused_kernel, n_dp), out_shape=jax.Shape...  56.8 us
    unnamed x23, local copies, waits for them, and re-layouts  10.5 us

profile of v1, /device:TPU:0, one launch (start us, length us, event | category | flops | bytes accessed | tf_op | source)
XLA Modules:
  0.0 68.2 jit_solution(7939530947091301379)
XLA Ops:
  0.0 0.8 %copy.12.seg_col_ref = s32[128,1]{1,0:T(8,128)S(1)} copy(s32[128,1]{0,1:T(1,128)} %bitcast.6) | data formatting | bytes 1024 | tf_op jit(solution)/shard_map/broadcast_in_dim | solution.py:542
  0.8 0.0 copy-start
  0.8 1.7 %copy-done = bf16[5120,256]{1,0:T(8,128)(2,1)S(1)} copy-done((bf16[5120,256]{1,0:T(8,128)(2,1)S(1)}, bf16[5120,256]{1,0:T(8,128)(2,1)}, u32[]{:S(2)}) %copy-start) | copy-done | bytes 2621464
  2.5 0.0 copy-start.1
  2.5 1.3 %copy-done.1 = bf16[128,5120]{1,0:T(8,128)(2,1)S(1)} copy-done((bf16[128,5120]{1,0:T(8,128)(2,1)S(1)}, bf16[128,5120]{1,0:T(8,128)(2,1)}, u32[]{:S(2)}) %copy-start.1) | copy-done | bytes 1310744
  3.8 0.0 copy-start.2
  3.8 1.1 %copy-done.2 = bf16[128,2560]{1,0:T(8,128)(2,1)S(1)} copy-done((bf16[128,2560]{1,0:T(8,128)(2,1)S(1)}, bf16[128,2560]{1,0:T(8,128)(2,1)}, u32[]{:S(2)}) %copy-start.2) | copy-done | bytes 655384
  4.9 0.0 copy-start.3
  4.9 0.9 %copy-done.3 = bf16[8,5120]{1,0:T(8,128)(2,1)S(1)} copy-done((bf16[8,5120]{1,0:T(8,128)(2,1)S(1)}, bf16[8,5120]{1,0:T(8,128)(2,1)}, u32[]{:S(2)}) %copy-start.3) | copy-done | bytes 81944
  5.8 0.0 copy-start.4
  5.8 0.7 %copy-done.4 = f32[5120]{0:T(1024)S(1)} copy-done((f32[5120]{0:T(1024)S(1)}, f32[5120]{0:T(1024)}, u32[]{:S(2)}) %copy-start.4) | copy-done | bytes 20504
  6.5 0.0 copy-start.5
  6.5 0.7 copy-done.5
  7.2 0.0 copy-start.6
  7.2 0.7 copy-done.6
  7.9 0.0 copy-start.7
  7.9 0.7 copy-done.7
  8.5 0.0 copy-start.8
  8.5 0.7 copy-done.8
  9.2 0.0 copy-start.9
  9.2 0.7 copy-done.9
  9.8 0.0 copy-start.10
  9.8 0.7 copy-done.10
  10.5 56.8 %shard_map.109 = bf16[128,2560]{1,0:T(8,128)(2,1)S(1)} custom-call(s32[1,16]{1,0:T(1,128)S(1)} %copy-done.7, s32[1,16]{1,0:T(1,128)S(1)} %copy-done.8, s32[1,16]{1,0:T(1,128)S(1)} %copy-done.9, s32[1,16]{1,0:T(1,128)S(1)} %copy-done.10, bf16[128,5120]{1,0:T(8,128)(2,1)S(1)} %copy-done.1, bf16[128,2560]{1,0:T(8,128)(2,1)S(1)} %copy-done.2, ...), custom_call_target="tpu_custom_call" | custom-call | flops 1342177280 | bytes 8388608 | tf_op jit(solution)/shard_map/pallas_call | solution.py:491
  67.3 0.8 %copy.14 = bf16[128,2560]{1,0:T(8,128)(2,1)} copy(bf16[128,2560]{1,0:T(8,128)(2,1)S(1)} %shard_map.109) | data formatting | bytes 1310720
Async XLA Ops:
  0.8 1.7 %copy-start = (bf16[5120,256]{1,0:T(8,128)(2,1)S(1)}, bf16[5120,256]{1,0:T(8,128)(2,1)}, u32[]{:S(2)}) copy-start(bf16[5120,256]{1,0:T(8,128)(2,1)} %weight_ref.1) | copy-start | bytes 7864324
  2.5 1.3 %copy-start.1 = (bf16[128,5120]{1,0:T(8,128)(2,1)S(1)}, bf16[128,5120]{1,0:T(8,128)(2,1)}, u32[]{:S(2)}) copy-start(bf16[128,5120]{1,0:T(8,128)(2,1)} %hidden_ref.1) | copy-start | bytes 3932164
  3.8 1.1 %copy-start.2 = (bf16[128,2560]{1,0:T(8,128)(2,1)S(1)}, bf16[128,2560]{1,0:T(8,128)(2,1)}, u32[]{:S(2)}) copy-start(bf16[128,2560]{1,0:T(8,128)(2,1)} %queries_ref.1) | copy-start | bytes 1966084
  4.9 0.9 %copy-start.3 = (bf16[8,5120]{1,0:T(8,128)(2,1)S(1)}, bf16[8,5120]{1,0:T(8,128)(2,1)}, u32[]{:S(2)}) copy-start(bf16[8,5120]{1,0:T(8,128)(2,1)} %table_ref.1) | copy-start | bytes 245764
  5.8 0.7 %copy-start.4 = (f32[5120]{0:T(1024)S(1)}, f32[5120]{0:T(1024)}, u32[]{:S(2)}) copy-start(f32[5120]{0:T(1024)} %param.14) | copy-start | bytes 61444
  6.5 0.7 copy-start.5
  7.2 0.7 copy-start.6
  7.9 0.7 copy-start.7
  8.5 0.7 copy-start.8
  9.2 0.7 copy-start.9
  9.8 0.7 copy-start.10

commit v2 on v1

--- a/solution.py
+++ b/solution.py
@@ -148,6 +148,7 @@
 
 MESH_ID = pl.DeviceIdType.MESH
 CHUNKS = 4
+VMEM_BYTES = 60 * 2**20
 
 
 def fused_kernel(
@@ -163,7 +164,6 @@
     weight_ref,
     bias_ref,
     seg_row_ref,
-    seg_col_ref,
     out_ref,
     weight,
     rows_held,
@@ -262,26 +262,37 @@
             rows_held.at[2, own], rows_held.at[3, own], f_send.at[c], f_recv.at[c], i, core_mate
         )
 
-    def q1_copy(o):
+    first_width = (q_width // HEAD_SIZE + 1) // 2 * HEAD_SIZE
+    pieces = ((0, first_width), (first_width, q_width - first_width))
+
+    def q1_source(head, piece):
+        at, width = pieces[piece]
+        return queries_ref.at[:, pl.ds(pl.multiple_of(head * q_width + at, HEAD_SIZE), width)]
+
+    def q1_copy(o, piece):
         head = lax.rem(i + o, n_dp)
-        cols = pl.ds(pl.multiple_of(head * q_width, 128), q_width)
-        return remote(
-            queries_ref.at[:, cols], q_first.at[i], q1_send.at[o], q1_recv.at[o], head, f
-        )
-
-    norm_part(0)
+        return remote(
+            q1_source(head, piece),
+            q_first.at[i, :, pl.ds(*pieces[piece])],
+            q1_send.at[o, piece],
+            q1_recv.at[o, piece],
+            head,
+            f,
+        )
+
+    def q1_own(piece):
+        return pltpu.make_async_copy(
+            q1_source(i, piece),
+            q_first.at[i, :, pl.ds(*pieces[piece])],
+            q1_recv.at[0, piece],
+        )
+
     pl.semaphore_wait(barrier, n_dp * 4 - 1)
-    x_copy(0).start()
-    c_copy(0).start()
-    q1_own = pltpu.make_async_copy(
-        queries_ref.at[:, pl.ds(pl.multiple_of(i * q_width, 128), q_width)],
-        q_first.at[i],
-        q1_recv.at[0],
-    )
-    q1_own.start()
-    for o in range(1, n_dp):
-        q1_copy(o).start()
-    for c in range(1, CHUNKS):
+    for piece in range(2):
+        for o in (2, 3, 1):
+            q1_copy(o, piece).start()
+        q1_own(piece).start()
+    for c in range(CHUNKS):
         norm_part(c)
         x_copy(c).start()
         c_copy(c).start()
@@ -349,10 +360,16 @@
         place = lax.broadcasted_iota(jnp.int32, (rows, every), 0) + block * rows
         return jnp.where(place == target, 1.0, 0.0).astype(jnp.bfloat16)
 
-    def q2_copy(o):
+    def q2_copy(o, piece):
         d = lax.rem(i + o, n_dp)
-        return remote(
-            q_perm.at[o], q_last.at[i], q2_send.at[o], q2_recv.at[o], d, f
+        cols = pl.ds(*pieces[piece])
+        return remote(
+            q_perm.at[o, :, cols],
+            q_last.at[i, :, cols],
+            q2_send.at[o, piece],
+            q2_recv.at[o, piece],
+            d,
+            f,
         )
 
     def kv2_copy(o):
@@ -361,20 +378,22 @@
             kv_perm.at[o], kv_last.at[i], kv2_send.at[o], kv2_recv.at[o], d, f
         )
 
-    def move_queries():
-        q1_own.wait()
+    def move_queries(piece):
+        q1_own(piece).wait()
         for o in range(1, n_dp):
-            q1_copy(o).wait_recv()
-        full = q_first[...].reshape(every, q_width)
+            q1_copy(o, piece).wait_recv()
+        at, width = pieces[piece]
+        cols = pl.ds(at, width)
+        full = q_first[:, :, cols].reshape(every, width)
         for o in (2, 3, 1, 0):
             moved = jnp.dot(
                 chosen(lax.rem(i + o, n_dp)), full, preferred_element_type=jnp.float32
             ).astype(jnp.bfloat16)
             if o:
-                q_perm[o] = moved
-                q2_copy(o).start()
+                q_perm[o, :, cols] = moved
+                q2_copy(o, piece).start()
             else:
-                q_last[i] = moved
+                q_last[i, :, cols] = moved
 
     for c in range(CHUNKS):
         c_copy(c).wait_recv()
@@ -384,13 +403,13 @@
     for c in range(CHUNKS):
         x_copy(c).wait_recv()
         f_copy(c).start()
-        if c == CHUNKS // 2:
-            move_queries()
         project_part(2, c * part, part)
         send_kv(2, c * part, part)
         f_copy(c).wait_recv()
         project_part(3, c * part, part)
         send_kv(3, c * part, part)
+        if c < 2:
+            move_queries(c)
 
     for a in range(n_dp):
         for t in range(2):
@@ -411,10 +430,11 @@
         if o:
             kv2_copy(o).start()
 
-    seg_col = seg_col_ref[...]
+    seg_row = jnp.broadcast_to(seg_row_ref[...].astype(jnp.float32), (rows, rows))
+    seg_col = jnp.transpose(seg_row)
     row_at = lax.broadcasted_iota(jnp.int32, (rows, rows), 0)
     col_at = lax.broadcasted_iota(jnp.int32, (rows, rows), 1)
-    allowed = (seg_col == seg_row_ref[...]) & (col_at <= row_at)
+    allowed = (seg_col == seg_row) & (col_at <= row_at)
     alive = seg_col >= 0
     heads = QUERY_HEADS // KEY_VALUE_HEADS
 
@@ -444,7 +464,8 @@
 
     attend_head(i)
     for o in (1, 3, 2):
-        q2_copy(o).wait_recv()
+        for piece in range(2):
+            q2_copy(o, piece).wait_recv()
         kv2_copy(o).wait_recv()
         attend_head(lax.rem(i + n_dp - o, n_dp))
 
@@ -453,8 +474,9 @@
         c_copy(c).wait_send()
         f_copy(c).wait_send()
     for o in range(1, n_dp):
-        q1_copy(o).wait_send()
-        q2_copy(o).wait_send()
+        for piece in range(2):
+            q1_copy(o, piece).wait_send()
+            q2_copy(o, piece).wait_send()
         kv2_copy(o).wait_send()
     for half in range(2):
         for slot in range(1, 4):
@@ -491,7 +513,7 @@
     return pl.pallas_call(
         functools.partial(fused_kernel, n_dp),
         out_shape=jax.ShapeDtypeStruct(queries.shape, bf16),
-        in_specs=[smem] * 4 + [vmem, anywhere, vmem, vmem, anywhere, vmem, vmem, vmem],
+        in_specs=[smem] * 4 + [vmem, anywhere, vmem, vmem, anywhere, vmem, vmem],
         out_specs=vmem,
         scratch_shapes=[
             pltpu.VMEM((model, columns), bf16),
@@ -510,17 +532,17 @@
             dma((CHUNKS,)),
             dma((CHUNKS,)),
             dma((CHUNKS,)),
-            dma((n_dp,)),
-            dma((n_dp,)),
+            dma((n_dp, 2)),
+            dma((n_dp, 2)),
             dma((4, 2)),
             dma((n_dp, 2)),
-            dma((n_dp,)),
-            dma((n_dp,)),
+            dma((n_dp, 2)),
+            dma((n_dp, 2)),
             dma((n_dp,)),
             dma((n_dp,)),
         ],
         compiler_params=pltpu.CompilerParams(
-            collective_id=0, has_side_effects=True, vmem_limit_bytes=40 * 2**20
+            collective_id=0, has_side_effects=True, vmem_limit_bytes=VMEM_BYTES
         ),
         cost_estimate=pl.CostEstimate(
             flops=2 * 4 * rows * model * columns,
@@ -539,7 +561,6 @@
         key_value_weight,
         value_projection_bias[None, :],
         segment_ids[None, :],
-        segment_ids[:, None],
     )
 
 

time: 68.6 us -> 55.7 us (0.81)
  local copies, waits for them, and re-layouts: 11.3 us -> 1.97 us
  Pallas kernels: 56.8 us -> 53.6 us
    unnamed x23 -> x1, local copies, waits for them, and re-layouts: 10.5 us -> 1.97 us
    pallas_call x1, Pallas kernels: 56.8 us -> 53.6 us  [fused_body(): pl.pallas_call(functools.partial(fused_kernel, n_dp), out_shape=jax.Shape...]
    broadcast_in_dim x1 -> x0, local copies, waits for them, and re-layouts: 0.76 us -> none  [fused_body(): segment_ids[:, None]]
where the time goes in v2:
time: 55.7 us; the launch traced here: 55.5 us
  Pallas kernels  53.6 us (96%)
  local copies, waits for them, and re-layouts  1.97 us (4%)
    pallas_call x1, Pallas kernels, fused_body(): pl.pallas_call(functools.partial(fused_kernel, n_dp), out_shape=jax.Shape...  53.6 us
    unnamed x1, local copies, waits for them, and re-layouts  1.97 us

profile of v2, /device:TPU:0, one launch (start us, length us, event | category | flops | bytes accessed | tf_op | source)
XLA Modules:
  0.0 55.5 jit_solution(12239189243068095155)
XLA Ops:
  0.0 53.6 %shard_map.109 = bf16[128,2560]{1,0:T(8,128)(2,1)} custom-call(s32[1,16]{1,0:T(1,128)} %lengths_ref.1, s32[1,16]{1,0:T(1,128)} %tags_ref.1, s32[1,16]{1,0:T(1,128)} %targets_ref.1, s32[1,16]{1,0:T(1,128)} %offsets_ref.1, bf16[128,5120]{1,0:T(8,128)(2,1)} %hidden_ref.1, bf16[128,2560]{1,0:T(8,128)(2,1)} %queries_ref.1, bf16[8,5120]{1,0:T(8,128)(2,1)} %table_ref.1, ...), custom_call_target="tpu_custom_call" | custom-call | flops 1342177280 | bytes 8388608 | tf_op jit(solution)/shard_map/pallas_call | solution.py:513
  53.6 2.0 %copy.13 = bf16[128,2560]{1,0:T(8,128)(2,1)} copy(bf16[128,2560]{1,0:T(8,128)(2,1)} %shard_map.109) | data formatting | bytes 1310720

commit v3 on v2

--- a/solution.py
+++ b/solution.py
@@ -148,6 +148,7 @@
 
 MESH_ID = pl.DeviceIdType.MESH
 CHUNKS = 4
+EARLY_CHUNK = 2
 VMEM_BYTES = 60 * 2**20
 
 
@@ -157,7 +158,7 @@
     tags_ref,
     targets_ref,
     offsets_ref,
-    hidden_ref,
+    hidden_from,
     queries_ref,
     table_ref,
     gain_ref,
@@ -165,6 +166,7 @@
     bias_ref,
     seg_row_ref,
     out_ref,
+    hidden_ref,
     weight,
     rows_held,
     kv_own,
@@ -174,6 +176,7 @@
     kv_perm,
     q_last,
     kv_last,
+    hidden_sem,
     weight_sem,
     x_send,
     x_recv,
@@ -190,7 +193,7 @@
     kv2_send,
     kv2_recv,
 ):
-    rows = hidden_ref.shape[0]
+    rows = hidden_from.shape[0]
     part = rows // CHUNKS
     every = n_dp * rows
     q_width = queries_ref.shape[1] // n_dp
@@ -212,7 +215,8 @@
         )
 
     load_weight = pltpu.make_async_copy(weight_ref, weight, weight_sem)
-    load_weight.start()
+    load_hidden = pltpu.make_async_copy(hidden_from, hidden_ref, hidden_sem)
+    load_hidden.start()
     barrier = pltpu.get_barrier_semaphore()
     for a in range(n_dp):
         for b in range(4):
@@ -287,11 +291,13 @@
             q1_recv.at[0, piece],
         )
 
+    load_weight.start()
     pl.semaphore_wait(barrier, n_dp * 4 - 1)
     for piece in range(2):
         for o in (2, 3, 1):
             q1_copy(o, piece).start()
         q1_own(piece).start()
+    load_hidden.wait()
     for c in range(CHUNKS):
         norm_part(c)
         x_copy(c).start()
@@ -372,11 +378,33 @@
             f,
         )
 
-    def kv2_copy(o):
+    def kv2_copy(o, t):
         d = lax.rem(i + o, n_dp)
         return remote(
-            kv_perm.at[o], kv_last.at[i], kv2_send.at[o], kv2_recv.at[o], d, f
-        )
+            kv_perm.at[o, t],
+            kv_last.at[i, t],
+            kv2_send.at[o, t],
+            kv2_recv.at[o, t],
+            d,
+            f,
+        )
+
+    def move_keys_or_values(t):
+        for a in range(n_dp):
+            landing = kv_first.at[t, pl.ds(a * rows, rows)]
+            remote(
+                landing, landing, kv1_send.at[0, 0], kv1_recv.at[a, t], i, x_mate
+            ).wait_recv()
+        full = kv_first[t]
+        for o in (2, 3, 1, 0):
+            moved = jnp.dot(
+                chosen(lax.rem(i + o, n_dp)), full, preferred_element_type=jnp.float32
+            ).astype(jnp.bfloat16)
+            if o:
+                kv_perm[o, t] = moved
+                kv2_copy(o, t).start()
+            else:
+                kv_last[i, t] = moved
 
     def move_queries(piece):
         q1_own(piece).wait()
@@ -410,32 +438,16 @@
         send_kv(3, c * part, part)
         if c < 2:
             move_queries(c)
-
-    for a in range(n_dp):
-        for t in range(2):
-            landing = kv_first.at[t, pl.ds(a * rows, rows)]
-            remote(
-                landing, landing, kv1_send.at[0, 0], kv1_recv.at[a, t], i, x_mate
-            ).wait_recv()
-    for o in (2, 3, 1, 0):
-        pick = chosen(lax.rem(i + o, n_dp))
-        for t in range(2):
-            moved = jnp.dot(pick, kv_first[t], preferred_element_type=jnp.float32).astype(
-                jnp.bfloat16
-            )
-            if o:
-                kv_perm[o, t] = moved
-            else:
-                kv_last[i, t] = moved
-        if o:
-            kv2_copy(o).start()
+        if c == EARLY_CHUNK:
+            move_keys_or_values(kind_of_half)
+
+    move_keys_or_values(1 - kind_of_half)
 
     seg_row = jnp.broadcast_to(seg_row_ref[...].astype(jnp.float32), (rows, rows))
     seg_col = jnp.transpose(seg_row)
     row_at = lax.broadcasted_iota(jnp.int32, (rows, rows), 0)
     col_at = lax.broadcasted_iota(jnp.int32, (rows, rows), 1)
     allowed = (seg_col == seg_row) & (col_at <= row_at)
-    alive = seg_col >= 0
     heads = QUERY_HEADS // KEY_VALUE_HEADS
 
     def attend_head(k):
@@ -457,7 +469,7 @@
             kv_last[k, 1],
             preferred_element_type=jnp.float32,
         ).reshape(heads, rows, HEAD_SIZE)
-        mixed = jnp.where(alive[None], mixed / totals, 0.0).astype(jnp.bfloat16)
+        mixed = (mixed / totals).astype(jnp.bfloat16)
         for h in range(heads):
             at = pl.multiple_of((k * heads + h) * HEAD_SIZE, HEAD_SIZE)
             out_ref[:, pl.ds(at, HEAD_SIZE)] = mixed[h]
@@ -466,7 +478,8 @@
     for o in (1, 3, 2):
         for piece in range(2):
             q2_copy(o, piece).wait_recv()
-        kv2_copy(o).wait_recv()
+        for t in range(2):
+            kv2_copy(o, t).wait_recv()
         attend_head(lax.rem(i + n_dp - o, n_dp))
 
     for c in range(CHUNKS):
@@ -477,7 +490,8 @@
         for piece in range(2):
             q1_copy(o, piece).wait_send()
             q2_copy(o, piece).wait_send()
-        kv2_copy(o).wait_send()
+        for t in range(2):
+            kv2_copy(o, t).wait_send()
     for half in range(2):
         for slot in range(1, 4):
             kv1_copy(slot, half, 0, rows).wait_send()
@@ -510,12 +524,13 @@
     anywhere = pl.BlockSpec(memory_space=pl.ANY)
     bf16 = jnp.bfloat16
     dma = pltpu.SemaphoreType.DMA
-    return pl.pallas_call(
+    attended = pl.pallas_call(
         functools.partial(fused_kernel, n_dp),
         out_shape=jax.ShapeDtypeStruct(queries.shape, bf16),
-        in_specs=[smem] * 4 + [vmem, anywhere, vmem, vmem, anywhere, vmem, vmem],
+        in_specs=[smem] * 4 + [anywhere, anywhere, vmem, vmem, anywhere, vmem, vmem],
         out_specs=vmem,
         scratch_shapes=[
+            pltpu.VMEM((rows, model), bf16),
             pltpu.VMEM((model, columns), bf16),
             pltpu.VMEM((4, rows, model), bf16),
             pltpu.VMEM((4, 2, rows, HEAD_SIZE), bf16),
@@ -525,6 +540,7 @@
             pltpu.VMEM((n_dp, 2, rows, HEAD_SIZE), bf16),
             pltpu.VMEM((n_dp, rows, q_width), bf16),
             pltpu.VMEM((n_dp, 2, rows, HEAD_SIZE), bf16),
+            dma,
             dma,
             dma((CHUNKS,)),
             dma((CHUNKS,)),
@@ -538,8 +554,8 @@
             dma((n_dp, 2)),
             dma((n_dp, 2)),
             dma((n_dp, 2)),
-            dma((n_dp,)),
-            dma((n_dp,)),
+            dma((n_dp, 2)),
+            dma((n_dp, 2)),
         ],
         compiler_params=pltpu.CompilerParams(
             collective_id=0, has_side_effects=True, vmem_limit_bytes=VMEM_BYTES
@@ -562,6 +578,7 @@
         value_projection_bias[None, :],
         segment_ids[None, :],
     )
+    return jnp.where(segment_ids[:, None] >= 0, attended, jnp.zeros((), bf16))
 
 
 def solution(mesh):

time: 55.7 us -> 56.2 us (level)
  other arithmetic: 0 us -> 2.7 us
  local copies, waits for them, and re-layouts: 1.97 us -> 0 us
    select_n x0 -> x1, other arithmetic: none -> 2.04 us  [fused_body(): return jnp.where(segment_ids[:, None] >= 0, attended, jnp.zeros((), bf16))]
    unnamed x1 -> x0, local copies, waits for them, and re-layouts: 1.97 us -> none
    ge x0 -> x1, other arithmetic: none -> 0.66 us  [fused_body(): return jnp.where(segment_ids[:, None] >= 0, attended, jnp.zeros((), bf16))]
where the time goes in v3:
time: 56.2 us; the launch traced here: 56 us
  Pallas kernels  53.3 us (95%)
  other arithmetic  2.7 us (5%)
    pallas_call x1, Pallas kernels, fused_body(): pl.pallas_call(functools.partial(fused_kernel, n_dp), out_shape=jax.Shape...  53.3 us
    select_n x1, other arithmetic, fused_body(): return jnp.where(segment_ids[:, None] >= 0, attended, jnp.zeros((), bf16))  2.04 us

profile of v3, /device:TPU:0, one launch (start us, length us, event | category | flops | bytes accessed | tf_op | source)
XLA Modules:
  0.0 56.0 jit_solution(6106574748224785142)
XLA Ops:
  0.0 0.7 %broadcast_compare_fusion = pred[128]{0:T(512)(128)(4,1)S(1)} fusion(s32[128]{0:T(128)} %param.21), kind=kLoop, calls=%fused_computation.1 | loop fusion | flops 128 | bytes 640 | tf_op jit(solution)/shard_map/ge | solution.py:581
  0.7 53.3 %shard_map.109 = bf16[128,2560]{1,0:T(8,128)(2,1)} custom-call(s32[1,16]{1,0:T(1,128)} %lengths_ref.1, s32[1,16]{1,0:T(1,128)} %tags_ref.1, s32[1,16]{1,0:T(1,128)} %targets_ref.1, s32[1,16]{1,0:T(1,128)} %offsets_ref.1, bf16[128,5120]{1,0:T(8,128)(2,1)} %hidden_from.1, bf16[128,2560]{1,0:T(8,128)(2,1)} %queries_ref.1, bf16[8,5120]{1,0:T(8,128)(2,1)} %table_ref.1, ...), custom_call_target="tpu_custom_call" | custom-call | flops 1342177280 | bytes 8388608 | tf_op jit(solution)/shard_map/pallas_call | solution.py:527
  53.9 2.0 %broadcast_select_fusion = bf16[128,2560]{1,0:T(8,128)(2,1)} fusion(bf16[128,2560]{1,0:T(8,128)(2,1)} %shard_map.109, pred[128]{0:T(512)(128)(4,1)S(1)} %broadcast_compare_fusion), kind=kLoop, calls=%fused_computation | loop fusion | flops 327680 | bytes 1310848 | tf_op jit(solution)/shard_map/jit(_where)/select_n | solution.py:581

commit v4 on v3

--- a/solution.py
+++ b/solution.py
@@ -316,6 +316,18 @@
         for half in range(2):
             kv_own[slot, half, own, :] = kv[:, half * HEAD_SIZE : (half + 1) * HEAD_SIZE]
 
+    def project_pair(first, count):
+        own = pl.ds(first, count)
+        both = jnp.concatenate([rows_held[2, own, :], rows_held[3, own, :]], axis=0)
+        product = jnp.dot(both, weight[...], preferred_element_type=jnp.float32)
+        kv = (product + bias).astype(jnp.bfloat16)
+        for slot in range(2):
+            for half in range(2):
+                kv_own[2 + slot, half, own, :] = kv[
+                    slot * count : (slot + 1) * count,
+                    half * HEAD_SIZE : (half + 1) * HEAD_SIZE,
+                ]
+
     def kv1_copy(slot, half, first, count):
         head = 2 * lax.rem(f, 2) + half
         landing = pl.ds(pl.multiple_of(i * rows + first, count), count)
@@ -431,10 +443,9 @@
     for c in range(CHUNKS):
         x_copy(c).wait_recv()
         f_copy(c).start()
-        project_part(2, c * part, part)
+        f_copy(c).wait_recv()
+        project_pair(c * part, part)
         send_kv(2, c * part, part)
-        f_copy(c).wait_recv()
-        project_part(3, c * part, part)
         send_kv(3, c * part, part)
         if c < 2:
             move_queries(c)
@@ -448,6 +459,7 @@
     row_at = lax.broadcasted_iota(jnp.int32, (rows, rows), 0)
     col_at = lax.broadcasted_iota(jnp.int32, (rows, rows), 1)
     allowed = (seg_col == seg_row) & (col_at <= row_at)
+    alive = seg_col >= 0
     heads = QUERY_HEADS // KEY_VALUE_HEADS
 
     def attend_head(k):
@@ -469,7 +481,7 @@
             kv_last[k, 1],
             preferred_element_type=jnp.float32,
         ).reshape(heads, rows, HEAD_SIZE)
-        mixed = (mixed / totals).astype(jnp.bfloat16)
+        mixed = jnp.where(alive[None], mixed / totals, 0.0).astype(jnp.bfloat16)
         for h in range(heads):
             at = pl.multiple_of((k * heads + h) * HEAD_SIZE, HEAD_SIZE)
             out_ref[:, pl.ds(at, HEAD_SIZE)] = mixed[h]
@@ -524,7 +536,7 @@
     anywhere = pl.BlockSpec(memory_space=pl.ANY)
     bf16 = jnp.bfloat16
     dma = pltpu.SemaphoreType.DMA
-    attended = pl.pallas_call(
+    return pl.pallas_call(
         functools.partial(fused_kernel, n_dp),
         out_shape=jax.ShapeDtypeStruct(queries.shape, bf16),
         in_specs=[smem] * 4 + [anywhere, anywhere, vmem, vmem, anywhere, vmem, vmem],
@@ -578,7 +590,6 @@
         value_projection_bias[None, :],
         segment_ids[None, :],
     )
-    return jnp.where(segment_ids[:, None] >= 0, attended, jnp.zeros((), bf16))
 
 
 def solution(mesh):

time: 56.2 us -> 55.5 us (0.988)
  other arithmetic: 2.7 us -> 0 us
  local copies, waits for them, and re-layouts: 0 us -> 1.97 us
    select_n x1 -> x0, other arithmetic: 2.04 us -> none  [fused_body(): return jnp.where(segment_ids[:, None] >= 0, attended, jnp.zeros((), bf16))]
    unnamed x0 -> x1, local copies, waits for them, and re-layouts: none -> 1.97 us
    ge x1 -> x0, other arithmetic: 0.66 us -> none  [fused_body(): return jnp.where(segment_ids[:, None] >= 0, attended, jnp.zeros((), bf16))]
where the time goes in v4:
time: 55.5 us; the launch traced here: 55.3 us
  Pallas kernels  53.3 us (96%)
  local copies, waits for them, and re-layouts  1.97 us (4%)
    pallas_call x1, Pallas kernels, fused_body(): pl.pallas_call(functools.partial(fused_kernel, n_dp), out_shape=jax.Shape...  53.3 us
    unnamed x1, local copies, waits for them, and re-layouts  1.97 us

profile of v4, /device:TPU:0, one launch (start us, length us, event | category | flops | bytes accessed | tf_op | source)
XLA Modules:
  0.0 55.3 jit_solution(3683713677235843661)
XLA Ops:
  0.0 53.3 %shard_map.109 = bf16[128,2560]{1,0:T(8,128)(2,1)} custom-call(s32[1,16]{1,0:T(1,128)} %lengths_ref.1, s32[1,16]{1,0:T(1,128)} %tags_ref.1, s32[1,16]{1,0:T(1,128)} %targets_ref.1, s32[1,16]{1,0:T(1,128)} %offsets_ref.1, bf16[128,5120]{1,0:T(8,128)(2,1)} %hidden_from.1, bf16[128,2560]{1,0:T(8,128)(2,1)} %queries_ref.1, bf16[8,5120]{1,0:T(8,128)(2,1)} %table_ref.1, ...), custom_call_target="tpu_custom_call" | custom-call | flops 1342177280 | bytes 8388608 | tf_op jit(solution)/shard_map/pallas_call | solution.py:539
  53.3 2.0 %copy.13 = bf16[128,2560]{1,0:T(8,128)(2,1)} copy(bf16[128,2560]{1,0:T(8,128)(2,1)} %shard_map.109) | data formatting | bytes 1310720
